TPU v7x, 32 devices: a whole 2x2x4 slice. The times are simulated.
32 devices in a mesh: ctx: 8 (over z, x), tp: 4 (over y, core).
Axes of the slice: x: 2, y: 2, z: 4, core: 2. Of those that a mesh axis runs over, the one named last changes fastest.
Arguments:
- queries: bfloat16 [2048, 8192], P('ctx', 'tp'), may hold values from -6 to 6
- key_proj: bfloat16 [2048, 8192], P('ctx', 'tp'), may hold values from -6 to 6
- values: bfloat16 [2048, 8192], P('ctx', 'tp'), may hold values from -6 to 6
- residues: float32 [16, 8192], P(None, 'tp'), may hold values from -0.4 to 0.4
- decay_rates: float32 [16, 8192], P(None, 'tp'), may hold values from 0 to 0.034, as said below
- skip_weight: float32 [8192], P('tp'), may hold values from 0.5 to 1.5
- stream: bfloat16 [2048, 8192], P('ctx', 'tp'), may hold values from -110 to 110
- norm_gain: float32 [8192], P('tp'), may hold values from 0.1 to 1.9
Outputs:
- new_stream: bfloat16 [2048, 8192], P('ctx', 'tp')
- normed: bfloat16 [2048, 8192], P('ctx', 'tp')
Inputs may be any that keep to these rules, and one draw needn't show every extreme that they name: `decay_rates`: each mode's decay per position; all positive.
All inputs are finite; a program needn't handle non-finite values.
Results may differ from a plain program's by a relative error of at most 0.007.
Values may be sent and summed in bfloat16 or wider, within the bound.
A program may use at most 128 MiB of HBM per device.

v0:
```python
import functools
import math

import jax
import jax.numpy as jnp
import numpy as np
from jax import lax
from jax.experimental import pallas as pl
from jax.experimental.pallas import tpu as pltpu
from jax.sharding import PartitionSpec as P

epsilon = 1e-06
lane = 128
sub = 8
dft_cols = 256
MESH = pl.DeviceIdType.MESH
f32 = jnp.float32
bf16 = jnp.bfloat16


def dft_tables(rows):
    freq = np.arange(rows)[:, None]
    pos = np.arange(rows)[None, :]
    angle = math.pi * (((2 * freq + 1) * pos) % (4 * rows)) / (2 * rows)
    forward = np.concatenate([np.cos(angle), -np.sin(angle)], axis=0)
    inverse = np.concatenate([np.cos(angle).T, -np.sin(angle).T], axis=1) / rows
    return forward.astype(bf16), inverse.astype(bf16)


def body(
    n_ctx, n_tp, n_sub, per_dev,
    q_hbm, k_hbm, v_hbm, res_hbm, dec_hbm, skip_hbm, str_hbm, gain_hbm, fwd_hbm, inv_hbm,
    new_hbm, norm_hbm,
    q, k, v, res, dec, skip, stream, gain, fwd, inv,
    sig, taps, conv, new, norm, ends, decay_pow, got, starts, states, square, row_sums,
    in_sem, out_sem, send1, recv1, send2, recv2, send3, recv3,
):
    rows, width = q.shape
    modes = res.shape[0]
    n_lane = width // lane
    part = modes // n_sub
    me = lax.axis_index("ctx")
    tp = lax.axis_index("tp")

    loads = {}
    order = [
        ("dec", dec_hbm, dec), ("q", q_hbm, q), ("k", k_hbm, k), ("res", res_hbm, res),
        ("fwd", fwd_hbm, fwd), ("inv", inv_hbm, inv), ("v", v_hbm, v),
        ("stream", str_hbm, stream), ("skip", skip_hbm, skip), ("gain", gain_hbm, gain),
    ]
    for i, (name, src, dst) in enumerate(order):
        loads[name] = pltpu.make_async_copy(src, dst, in_sem.at[i])
        loads[name].start()

    barrier = pltpu.get_barrier_semaphore()
    for d in range(1, n_ctx):
        pl.semaphore_signal(barrier, inc=1, device_id={"ctx": lax.rem(me + d, n_ctx)}, device_id_type=MESH)
    for d in range(1, n_tp):
        pl.semaphore_signal(barrier, inc=1, device_id={"tp": lax.rem(tp + d, n_tp)}, device_id_type=MESH)

    sublane = lax.broadcasted_iota(jnp.int32, (sub, lane), 0).astype(f32)

    def lanes_of(t):
        return pl.ds(pl.multiple_of(t * lane, lane), lane)

    def spread(x, n):
        return jnp.broadcast_to(x[n:n + 1, :], (sub, lane))

    for name in ("dec", "q", "k"):
        loads[name].wait()

    def end_states(t, _):
        cols = lanes_of(t)
        rate = dec[:, cols]
        step = jnp.exp(rate * (-float(sub)))
        steps = [spread(step, n) for n in range(modes)]

        def block(m, acc):
            at = pl.ds(pl.multiple_of(m * 16, 16), 16)
            s = (q[at, cols].astype(f32) * k[at, cols].astype(f32)).astype(bf16)
            sig[at, cols] = s
            s = s.astype(f32)
            acc = tuple(a * b + s[:8] for a, b in zip(acc, steps))
            return tuple(a * b + s[8:] for a, b in zip(acc, steps))

        acc = lax.fori_loop(0, rows // 16, block, (jnp.zeros((sub, lane), f32),) * modes, unroll=4)
        total = jnp.concatenate(
            [
                jnp.sum(a * jnp.exp(-spread(rate, n) * (sub - 1.0 - sublane)), axis=0, keepdims=True)
                for n, a in enumerate(acc)
            ],
            axis=0,
        )
        power = jnp.exp(rate * (-float(rows)))
        for g in range(n_sub):
            ends[t * n_sub + g] = total[g * part:(g + 1) * part]
            decay_pow[t * n_sub + g] = power[g * part:(g + 1) * part]
        return 0

    lax.fori_loop(0, n_lane, end_states, 0)

    pl.semaphore_wait(barrier, n_ctx - 1 + n_tp - 1)

    mine = pl.ds(me * per_dev, per_dev)
    first = []
    for d in range(1, n_ctx):
        to = lax.rem(me + d, n_ctx)
        copy = pltpu.make_async_remote_copy(
            src_ref=ends.at[pl.ds(to * per_dev, per_dev)], dst_ref=got.at[me],
            send_sem=send1.at[d], recv_sem=recv1.at[d], device_id={"ctx": to}, device_id_type=MESH,
        )
        copy.start()
        first.append(copy)

    def modal(coefs, steps, emit):
        def block(m, z):
            top = sum(z[1:], z[0])
            z = tuple(a * b for a, b in zip(z, steps))
            low = sum(z[1:], z[0])
            z = tuple(a * b for a, b in zip(z, steps))
            emit(pl.ds(pl.multiple_of(m * 16, 16), 16), jnp.concatenate([top, low], axis=0))
            return z

        lax.fori_loop(0, rows // 16, block, tuple(coefs), unroll=4)

    loads["res"].wait()

    def make_taps(t, _):
        cols = lanes_of(t)
        rate = dec[:, cols]
        weight = res[:, cols]
        step = jnp.exp(rate * (-float(sub)))
        steps = [spread(step, n) for n in range(modes)]
        coefs = [spread(weight, n) * jnp.exp(-spread(rate, n) * sublane) for n in range(modes)]

        def emit(at, value):
            taps[at, cols] = value.astype(bf16)

        modal(coefs, steps, emit)
        return 0

    lax.fori_loop(0, n_lane, make_taps, 0)

    for d, copy in enumerate(first, 1):
        pltpu.make_async_remote_copy(
            src_ref=ends.at[mine], dst_ref=got.at[lax.rem(me - d + n_ctx, n_ctx)],
            send_sem=send1.at[d], recv_sem=recv1.at[d], device_id={"ctx": me}, device_id_type=MESH,
        ).wait_recv()
    got[me] = ends[mine]
    power = decay_pow[mine]
    running = jnp.zeros_like(power)
    for j in range(n_ctx):
        starts[j] = running
        running = running * power + got[j]

    second = []
    for d in range(1, n_ctx):
        to = lax.rem(me + d, n_ctx)
        copy = pltpu.make_async_remote_copy(
            src_ref=starts.at[to], dst_ref=states.at[mine],
            send_sem=send2.at[d], recv_sem=recv2.at[d], device_id={"ctx": to}, device_id_type=MESH,
        )
        copy.start()
        second.append(copy)
    states[mine] = starts[me]

    loads["fwd"].wait()
    loads["inv"].wait()

    def local_conv(c, _):
        cols = pl.ds(pl.multiple_of(c * dft_cols, dft_cols), dft_cols)
        u = jnp.dot(fwd[...], sig[:, cols], preferred_element_type=f32)
        h = jnp.dot(fwd[...], taps[:, cols], preferred_element_type=f32)
        ur, ui, hr, hi = u[:rows], u[rows:], h[:rows], h[rows:]
        prod = jnp.concatenate([ur * hr - ui * hi, ur * hi + ui * hr], axis=0).astype(bf16)
        conv[:, cols] = jnp.dot(inv[...], prod, preferred_element_type=f32)
        return 0

    lax.fori_loop(0, width // dft_cols, local_conv, 0)

    for name in ("v", "stream", "skip", "gain"):
        loads[name].wait()
    square[...] = jnp.zeros_like(square)

    for d in range(1, n_ctx):
        frm = lax.rem(me - d + n_ctx, n_ctx)
        pltpu.make_async_remote_copy(
            src_ref=starts.at[me], dst_ref=states.at[pl.ds(frm * per_dev, per_dev)],
            send_sem=send2.at[d], recv_sem=recv2.at[d], device_id={"ctx": me}, device_id_type=MESH,
        ).wait_recv()

    def finish(t, _):
        cols = lanes_of(t)
        rate = dec[:, cols]
        state = jnp.concatenate([states[t * n_sub + g] for g in range(n_sub)], axis=0)
        weight = res[:, cols] * state
        step = jnp.exp(rate * (-float(sub)))
        steps = [spread(step, n) for n in range(modes)]
        coefs = [spread(weight, n) * jnp.exp(-spread(rate, n) * (sublane + 1.0)) for n in range(modes)]
        direct = skip[:, cols]

        def emit(at, value):
            value = value + conv[at, cols] + direct * sig[at, cols].astype(f32)
            out = (stream[at, cols].astype(f32) + v[at, cols].astype(f32) * value).astype(bf16)
            new[at, cols] = out
            out = out.astype(f32)
            square[at, :] += out * out

        modal(coefs, steps, emit)
        return 0

    lax.fori_loop(0, n_lane, finish, 0)
    write_new = pltpu.make_async_copy(new, new_hbm, out_sem.at[0])
    write_new.start()

    ones = jnp.ones((sub, lane), f32)
    row_sums[tp] = lax.dot_general(
        ones, square[...], (((1,), (1,)), ((), ())),
        precision=lax.Precision.HIGHEST, preferred_element_type=f32,
    )
    third = []
    for d in range(1, n_tp):
        to = lax.rem(tp + d, n_tp)
        copy = pltpu.make_async_remote_copy(
            src_ref=row_sums.at[tp], dst_ref=row_sums.at[tp],
            send_sem=send3.at[d], recv_sem=recv3.at[d], device_id={"tp": to}, device_id_type=MESH,
        )
        copy.start()
        third.append(copy)
    for d in range(1, n_tp):
        frm = lax.rem(tp - d + n_tp, n_tp)
        pltpu.make_async_remote_copy(
            src_ref=row_sums.at[tp], dst_ref=row_sums.at[frm],
            send_sem=send3.at[d], recv_sem=recv3.at[d], device_id={"tp": tp}, device_id_type=MESH,
        ).wait_recv()
    total = row_sums[0]
    for j in range(1, n_tp):
        total = total + row_sums[j]
    mean = lax.dot_general(
        total, jnp.full((sub, lane), 1.0 / sub, f32), (((0,), (0,)), ((), ())),
        precision=lax.Precision.HIGHEST, preferred_element_type=f32,
    ) / (width * n_tp)
    square[...] = lax.rsqrt(mean + epsilon)

    def scale(t, _):
        cols = lanes_of(t)
        norm[:, cols] = (new[:, cols].astype(f32) * square[...] * gain[:, cols]).astype(bf16)
        return 0

    lax.fori_loop(0, n_lane, scale, 0)
    write_norm = pltpu.make_async_copy(norm, norm_hbm, out_sem.at[1])
    write_norm.start()
    for copy in first + second + third:
        copy.wait_send()
    write_new.wait()
    write_norm.wait()


def shards(n_ctx, n_tp, queries, key_proj, values, residues, decay_rates, skip_weight, stream, norm_gain):
    rows, width = queries.shape
    modes = residues.shape[0]
    n_lane = width // lane
    n_sub = max(1, n_ctx // n_lane)
    part = modes // n_sub
    blocks = n_lane * n_sub
    per_dev = blocks // n_ctx
    assert per_dev * n_ctx == blocks and part * n_sub == modes
    forward, inverse = dft_tables(rows)
    slab = pltpu.VMEM((rows, width), bf16)
    wide = pltpu.VMEM((modes, width), f32)
    line = pltpu.VMEM((1, width), f32)
    dma = pltpu.SemaphoreType.DMA
    whole = pl.BlockSpec(memory_space=pl.ANY)
    out = jax.ShapeDtypeStruct((rows, width), bf16)
    return pl.pallas_call(
        functools.partial(body, n_ctx, n_tp, n_sub, per_dev),
        out_shape=(out, out),
        in_specs=[whole] * 10,
        out_specs=(whole, whole),
        scratch_shapes=[
            slab, slab, slab, wide, wide, line, slab, line,
            pltpu.VMEM((2 * rows, rows), bf16), pltpu.VMEM((rows, 2 * rows), bf16),
            slab, slab, pltpu.VMEM((rows, width), f32), slab, slab,
            pltpu.VMEM((blocks, part, lane), f32),
            pltpu.VMEM((blocks, part, lane), f32),
            pltpu.VMEM((n_ctx, per_dev, part, lane), f32),
            pltpu.VMEM((n_ctx, per_dev, part, lane), f32),
            pltpu.VMEM((blocks, part, lane), f32),
            pltpu.VMEM((rows, lane), f32),
            pltpu.VMEM((n_tp, sub, rows), f32),
            dma((10,)), dma((2,)),
            dma((n_ctx,)), dma((n_ctx,)), dma((n_ctx,)), dma((n_ctx,)), dma((n_tp,)), dma((n_tp,)),
        ],
        compiler_params=pltpu.CompilerParams(
            collective_id=0, has_side_effects=True, vmem_limit_bytes=48 * 1024 * 1024
        ),
        cost_estimate=pl.CostEstimate(
            flops=6 * rows * rows * width * 2, bytes_accessed=6 * rows * width * 2, transcendentals=0
        ),
    )(
        queries, key_proj, values, residues, decay_rates, skip_weight[None, :], stream,
        norm_gain[None, :], jnp.asarray(forward), jnp.asarray(inverse),
    )


def solution(mesh):
    in_specs = (
        P("ctx", "tp"),
        P("ctx", "tp"),
        P("ctx", "tp"),
        P(None, "tp"),
        P(None, "tp"),
        P("tp"),
        P("ctx", "tp"),
        P("tp"),
    )
    out_specs = (P("ctx", "tp"), P("ctx", "tp"))
    return jax.shard_map(
        functools.partial(shards, mesh.shape["ctx"], mesh.shape["tp"]),
        mesh=mesh, in_specs=in_specs, out_specs=out_specs, check_vma=False,
    )
```

profile of v0, /device:TPU:0, one launch (start us, length us, event | category | flops | bytes accessed | tf_op | source)
XLA Modules:
  0.0 38.4 jit_solution(5021324404571804926)
XLA Ops:
  0.6 0.0 copy-start
  0.6 1.2 %copy-done = bf16[256,2048]{1,0:T(8,128)(2,1)S(1)} copy-done((bf16[256,2048]{1,0:T(8,128)(2,1)S(1)}, bf16[256,2048]{1,0:T(8,128)(2,1)}, u32[]{:S(2)}) %copy-start) | copy-done | bytes 1048600
  1.9 0.0 copy-start.1
  1.9 1.2 %copy-done.1 = bf16[256,2048]{1,0:T(8,128)(2,1)S(1)} copy-done((bf16[256,2048]{1,0:T(8,128)(2,1)S(1)}, bf16[256,2048]{1,0:T(8,128)(2,1)}, u32[]{:S(2)}) %copy-start.1) | copy-done | bytes 1048600
  3.1 0.0 copy-start.2
  3.1 1.2 %copy-done.2 = bf16[256,2048]{1,0:T(8,128)(2,1)S(1)} copy-done((bf16[256,2048]{1,0:T(8,128)(2,1)S(1)}, bf16[256,2048]{1,0:T(8,128)(2,1)}, u32[]{:S(2)}) %copy-start.2) | copy-done | bytes 1048600
  4.3 0.0 copy-start.3
  4.3 0.9 %copy-done.3 = f32[16,2048]{1,0:T(8,128)S(1)} copy-done((f32[16,2048]{1,0:T(8,128)S(1)}, f32[16,2048]{1,0:T(8,128)}, u32[]{:S(2)}) %copy-start.3) | copy-done | bytes 131096
  5.2 0.0 copy-start.4
  5.2 0.9 %copy-done.4 = f32[16,2048]{1,0:T(8,128)S(1)} copy-done((f32[16,2048]{1,0:T(8,128)S(1)}, f32[16,2048]{1,0:T(8,128)}, u32[]{:S(2)}) %copy-start.4) | copy-done | bytes 131096
  6.1 0.0 copy-start.5
  6.1 0.7 %copy-done.5 = f32[2048]{0:T(1024)S(1)} copy-done((f32[2048]{0:T(1024)S(1)}, f32[2048]{0:T(1024)}, u32[]{:S(2)}) %copy-start.5) | copy-done | bytes 8216
  6.8 0.0 copy-start.6
  6.8 0.7 %copy-done.6 = f32[2048]{0:T(1024)S(1)} copy-done((f32[2048]{0:T(1024)S(1)}, f32[2048]{0:T(1024)}, u32[]{:S(2)}) %copy-start.6) | copy-done | bytes 8216
  7.5 0.0 copy-start.7
  7.5 0.9 %copy-done.7 = bf16[256,512]{1,0:T(8,128)(2,1)S(1)} copy-done((bf16[256,512]{1,0:T(8,128)(2,1)S(1)}, bf16[256,512]{1,0:T(8,128)(2,1)}, u32[]{:S(2)}) %copy-start.7) | copy-done | bytes 262168
  8.5 0.0 copy-start.8
  8.5 0.9 %copy-done.8 = bf16[512,256]{1,0:T(8,128)(2,1)S(1)} copy-done((bf16[512,256]{1,0:T(8,128)(2,1)S(1)}, bf16[512,256]{1,0:T(8,128)(2,1)}, u32[]{:S(2)}) %copy-start.8) | copy-done | bytes 262168
  9.4 27.0 %shard_map.113 = (bf16[256,2048]{1,0:T(8,128)(2,1)S(1)}, bf16[256,2048]{1,0:T(8,128)(2,1)S(1)}) custom-call(bf16[256,2048]{1,0:T(8,128)(2,1)S(1)} %copy-done, bf16[256,2048]{1,0:T(8,128)(2,1)S(1)} %copy-done.1, bf16[256,2048]{1,0:T(8,128)(2,1)S(1)} %copy-done.2, f32[16,2048]{1,0:T(8,128)S(1)} %copy-done.3, f32[16,2048]{1,0:T(8,128)S(1)} %copy-done.4, ...), custom_call_target="tpu_custom_call" | custom-call | flops 1610612736 | bytes 6291456 | tf_op jit(solution)/shard_map/pallas_call | solution.py:275
  36.4 1.0 %copy.14 = bf16[256,2048]{1,0:T(8,128)(2,1)} copy(bf16[256,2048]{1,0:T(8,128)(2,1)S(1)} %get-tuple-element.4) | data formatting | bytes 2097152
  37.4 1.0 %copy.15 = bf16[256,2048]{1,0:T(8,128)(2,1)} copy(bf16[256,2048]{1,0:T(8,128)(2,1)S(1)} %get-tuple-element.5) | data formatting | bytes 2097152
Async XLA Ops:
  0.6 1.2 %copy-start = (bf16[256,2048]{1,0:T(8,128)(2,1)S(1)}, bf16[256,2048]{1,0:T(8,128)(2,1)}, u32[]{:S(2)}) copy-start(bf16[256,2048]{1,0:T(8,128)(2,1)} %q_hbm.1) | copy-start | bytes 3145732
  1.9 1.2 %copy-start.1 = (bf16[256,2048]{1,0:T(8,128)(2,1)S(1)}, bf16[256,2048]{1,0:T(8,128)(2,1)}, u32[]{:S(2)}) copy-start(bf16[256,2048]{1,0:T(8,128)(2,1)} %k_hbm.1) | copy-start | bytes 3145732
  3.1 1.2 %copy-start.2 = (bf16[256,2048]{1,0:T(8,128)(2,1)S(1)}, bf16[256,2048]{1,0:T(8,128)(2,1)}, u32[]{:S(2)}) copy-start(bf16[256,2048]{1,0:T(8,128)(2,1)} %v_hbm.1) | copy-start | bytes 3145732
  4.3 0.9 %copy-start.3 = (f32[16,2048]{1,0:T(8,128)S(1)}, f32[16,2048]{1,0:T(8,128)}, u32[]{:S(2)}) copy-start(f32[16,2048]{1,0:T(8,128)} %res_hbm.1) | copy-start | bytes 393220
  5.2 0.9 %copy-start.4 = (f32[16,2048]{1,0:T(8,128)S(1)}, f32[16,2048]{1,0:T(8,128)}, u32[]{:S(2)}) copy-start(f32[16,2048]{1,0:T(8,128)} %dec_hbm.1) | copy-start | bytes 393220
  6.1 0.7 %copy-start.5 = (f32[2048]{0:T(1024)S(1)}, f32[2048]{0:T(1024)}, u32[]{:S(2)}) copy-start(f32[2048]{0:T(1024)} %param.15) | copy-start | bytes 24580
  6.8 0.7 %copy-start.6 = (f32[2048]{0:T(1024)S(1)}, f32[2048]{0:T(1024)}, u32[]{:S(2)}) copy-start(f32[2048]{0:T(1024)} %param.17) | copy-start | bytes 24580
  7.5 0.9 %copy-start.7 = (bf16[256,512]{1,0:T(8,128)(2,1)S(1)}, bf16[256,512]{1,0:T(8,128)(2,1)}, u32[]{:S(2)}) copy-start(bf16[256,512]{1,0:T(8,128)(2,1)} %constant.5.clone.inv_hbm) | copy-start | bytes 786436
  8.5 0.9 %copy-start.8 = (bf16[512,256]{1,0:T(8,128)(2,1)S(1)}, bf16[512,256]{1,0:T(8,128)(2,1)}, u32[]{:S(2)}) copy-start(bf16[512,256]{1,0:T(8,128)(2,1)} %constant.4.clone.fwd_hbm) | copy-start | bytes 786436
where the time goes:
time: 38.8 us; the launch traced here: 38.4 us
  Pallas kernels  27 us (70%)
  local copies, waits for them, and re-layouts  10.7 us (28%)
  between operations  0.66 us (2%)
    pallas_call x1, Pallas kernels, shards(): pl.pallas_call(functools.partial(body, n_ctx, n_tp, n_sub, per_dev), out_...  27 us
    unnamed x20, local copies, waits for them, and re-layouts  10.7 us

commit v1 on v0

v1 whole, which is shorter than its diff:
```python
import functools
import math

import jax
import jax.numpy as jnp
import numpy as np
from jax import lax
from jax.experimental import pallas as pl
from jax.experimental.pallas import tpu as pltpu
from jax.sharding import PartitionSpec as P

epsilon = 1e-06
lane = 128
sub = 8
dft_cols = 256
MESH = pl.DeviceIdType.MESH
f32 = jnp.float32
bf16 = jnp.bfloat16


def dft_tables(rows):
    freq = np.arange(rows)[:, None]
    pos = np.arange(rows)[None, :]
    angle = math.pi * (((2 * freq + 1) * pos) % (4 * rows)) / (2 * rows)
    forward = np.concatenate([np.cos(angle), -np.sin(angle)], axis=0)
    inverse = np.concatenate([np.cos(angle).T, -np.sin(angle).T], axis=1) / rows
    return np.ascontiguousarray(forward.astype(bf16)), np.ascontiguousarray(inverse.astype(bf16))


def body(
    n_ctx, n_tp, n_sub, per_dev, chunk,
    q_hbm, k_hbm, v_hbm, res_hbm, dec_hbm, skip_hbm, str_hbm, fwd_hbm, inv_hbm,
    new, inv_rms,
    q, k, v, res, dec, skip, stream, fwd, inv,
    sig, taps, conv, ends, mids, decay_pow, got, starts, states, square, row_sums,
    in_sem, send1, recv1, send2, recv2, send3, recv3,
):
    rows, width = q.shape
    modes = res.shape[0]
    n_lane = width // lane
    n_chunk = rows // chunk
    part = modes // n_sub
    me = lax.axis_index("ctx")
    tp = lax.axis_index("tp")

    loads = {}
    order = [
        ("dec", dec_hbm, dec), ("q", q_hbm, q), ("k", k_hbm, k), ("res", res_hbm, res),
        ("fwd", fwd_hbm, fwd), ("inv", inv_hbm, inv), ("v", v_hbm, v),
        ("stream", str_hbm, stream), ("skip", skip_hbm, skip),
    ]
    for i, (name, src, dst) in enumerate(order):
        loads[name] = pltpu.make_async_copy(src, dst, in_sem.at[i])
        loads[name].start()

    barrier = pltpu.get_barrier_semaphore()
    for d in range(1, n_ctx):
        pl.semaphore_signal(barrier, inc=1, device_id={"ctx": lax.rem(me + d, n_ctx)}, device_id_type=MESH)
    for d in range(1, n_tp):
        pl.semaphore_signal(barrier, inc=1, device_id={"tp": lax.rem(tp + d, n_tp)}, device_id_type=MESH)

    sublane = lax.broadcasted_iota(jnp.int32, (sub, lane), 0).astype(f32)

    def lanes_of(t):
        return pl.ds(pl.multiple_of(t * lane, lane), lane)

    def spread(x, n):
        return jnp.broadcast_to(x[n:n + 1, :], (sub, lane))

    def rows_of(h, m):
        return pl.ds(pl.multiple_of(h * chunk + m * 16, 16), 16)

    for name in ("dec", "q", "k"):
        loads[name].wait()

    def end_states(t):
        cols = lanes_of(t)
        rate = dec[:, cols]
        step = jnp.exp(rate * (-float(sub)))
        steps = [spread(step, n) for n in range(modes)]
        tails = [jnp.exp(-spread(rate, n) * (sub - 1.0 - sublane)) for n in range(modes)]
        acc = (jnp.zeros((sub, lane), f32),) * modes
        for h in range(n_chunk):

            def block(m, acc):
                at = rows_of(h, m)
                s = (q[at, cols].astype(f32) * k[at, cols].astype(f32)).astype(bf16)
                sig[at, cols] = s
                s = s.astype(f32)
                acc = tuple(a * b + s[:8] for a, b in zip(acc, steps))
                return tuple(a * b + s[8:] for a, b in zip(acc, steps))

            acc = lax.fori_loop(0, chunk // 16, block, acc, unroll=True)
            total = jnp.concatenate(
                [jnp.sum(a * w, axis=0, keepdims=True) for a, w in zip(acc, tails)], axis=0
            )
            if h < n_chunk - 1:
                mids[h, t] = total
        power = jnp.exp(rate * (-float(rows)))
        for g in range(n_sub):
            ends[t * n_sub + g] = total[g * part:(g + 1) * part]
            decay_pow[t * n_sub + g] = power[g * part:(g + 1) * part]

    def loop(first, last, step):
        def run(i, _):
            step(i)
            return 0

        lax.fori_loop(first, last, run, 0)

    mine = pl.ds(me * per_dev, per_dev)

    def copy_ends(d):
        to = lax.rem(me + d, n_ctx)
        return pltpu.make_async_remote_copy(
            src_ref=ends.at[pl.ds(to * per_dev, per_dev)], dst_ref=got.at[me],
            send_sem=send1.at[d], recv_sem=recv1.at[d], device_id={"ctx": to}, device_id_type=MESH,
        )

    if n_sub == 1:
        def share(d):
            loop(0, per_dev, lambda i: end_states(lax.rem(me + d, n_ctx) * per_dev + i))

        share(1)
        pl.semaphore_wait(barrier, n_ctx - 1 + n_tp - 1)
        copy_ends(1).start()

        def share_and_send(d):
            share(d)
            copy_ends(d).start()

        loop(2, n_ctx, share_and_send)
        share(0)
    else:
        loop(0, n_lane, end_states)
        pl.semaphore_wait(barrier, n_ctx - 1 + n_tp - 1)
        loop(1, n_ctx, lambda d: copy_ends(d).start())

    def modal(h, coefs, steps, emit):
        def block(m, z):
            top = sum(z[1:], z[0])
            z = tuple(a * b for a, b in zip(z, steps))
            low = sum(z[1:], z[0])
            z = tuple(a * b for a, b in zip(z, steps))
            emit(rows_of(h, m), jnp.concatenate([top, low], axis=0))
            return z

        lax.fori_loop(0, chunk // 16, block, tuple(coefs), unroll=True)

    loads["res"].wait()

    def make_taps(t):
        cols = lanes_of(t)
        rate = dec[:, cols]
        weight = res[:, cols]
        step = jnp.exp(rate * (-float(sub)))
        steps = [spread(step, n) for n in range(modes)]
        coefs = [spread(weight, n) * jnp.exp(-spread(rate, n) * sublane) for n in range(modes)]

        def emit(at, value):
            taps[at, cols] = value.astype(bf16)

        modal(0, coefs, steps, emit)

    loop(0, n_lane, make_taps)

    loop(1, n_ctx, lambda d: copy_ends(d).wait_recv())
    got[me] = ends[mine]
    power = decay_pow[mine]
    running = jnp.zeros_like(power)
    for j in range(n_ctx):
        starts[j] = running
        running = running * power + got[j]

    def copy_starts(d):
        to = lax.rem(me + d, n_ctx)
        return pltpu.make_async_remote_copy(
            src_ref=starts.at[to], dst_ref=states.at[mine],
            send_sem=send2.at[d], recv_sem=recv2.at[d], device_id={"ctx": to}, device_id_type=MESH,
        )

    loop(1, n_ctx, lambda d: copy_starts(d).start())
    states[mine] = starts[me]

    loads["fwd"].wait()
    loads["inv"].wait()

    def local_conv(c):
        cols = pl.ds(pl.multiple_of(c * dft_cols, dft_cols), dft_cols)
        g = jnp.dot(fwd[...], taps[:, cols], preferred_element_type=f32)
        gr, gi = g[:chunk], g[chunk:]
        for h in range(n_chunk):
            at = pl.ds(h * chunk, chunk)
            u = jnp.dot(fwd[...], sig[at, cols], preferred_element_type=f32)
            ur, ui = u[:chunk], u[chunk:]
            prod = jnp.concatenate([ur * gr - ui * gi, ur * gi + ui * gr], axis=0).astype(bf16)
            conv[at, cols] = jnp.dot(inv[...], prod, preferred_element_type=f32)

    loop(0, width // dft_cols, local_conv)

    for name in ("v", "stream", "skip"):
        loads[name].wait()
    square[...] = jnp.zeros_like(square)

    def finish(t):
        cols = lanes_of(t)
        rate = dec[:, cols]
        state = jnp.concatenate([states[t * n_sub + g] for g in range(n_sub)], axis=0)
        weight = res[:, cols]
        step = jnp.exp(rate * (-float(sub)))
        steps = [spread(step, n) for n in range(modes)]
        heads = [jnp.exp(-spread(rate, n) * (sublane + 1.0)) for n in range(modes)]
        direct = skip[:, cols]

        def emit(at, value):
            value = value + conv[at, cols] + direct * sig[at, cols].astype(f32)
            out = (stream[at, cols].astype(f32) + v[at, cols].astype(f32) * value).astype(bf16)
            new[at, cols] = out
            out = out.astype(f32)
            square[at, :] += out * out

        for h in range(n_chunk):
            now = state if h == 0 else state * jnp.exp(rate * (-float(h * chunk))) + mids[h - 1, t]
            now = now * weight
            modal(h, [spread(now, n) * w for n, w in enumerate(heads)], steps, emit)

    if n_sub == 1:
        def finish_share(d):
            frm = lax.rem(me - d + n_ctx, n_ctx)
            loop(0, per_dev, lambda i: finish(frm * per_dev + i))

        def wait_and_finish(d):
            frm = lax.rem(me - d + n_ctx, n_ctx)
            pltpu.make_async_remote_copy(
                src_ref=starts.at[me], dst_ref=states.at[pl.ds(frm * per_dev, per_dev)],
                send_sem=send2.at[d], recv_sem=recv2.at[d], device_id={"ctx": frm}, device_id_type=MESH,
            ).wait_recv()
            finish_share(d)

        finish_share(0)
        loop(1, n_ctx, wait_and_finish)
    else:
        loop(1, n_ctx, lambda d: copy_starts(d).wait_recv())
        loop(0, n_lane, finish)

    ones = jnp.ones((sub, lane), f32)
    row_sums[tp] = lax.dot_general(
        ones, square[...], (((1,), (1,)), ((), ())),
        precision=lax.Precision.HIGHEST, preferred_element_type=f32,
    )
    third = []
    for d in range(1, n_tp):
        to = lax.rem(tp + d, n_tp)
        copy = pltpu.make_async_remote_copy(
            src_ref=row_sums.at[tp], dst_ref=row_sums.at[tp],
            send_sem=send3.at[d], recv_sem=recv3.at[d], device_id={"tp": to}, device_id_type=MESH,
        )
        copy.start()
        third.append(copy)
    loop(1, n_ctx, lambda d: copy_ends(d).wait_send())
    loop(1, n_ctx, lambda d: copy_starts(d).wait_send())
    for copy in third:
        copy.wait_recv()
    total = row_sums[0]
    for j in range(1, n_tp):
        total = total + row_sums[j]
    mean = lax.dot_general(
        total, jnp.full((sub, lane), 1.0 / sub, f32), (((0,), (0,)), ((), ())),
        precision=lax.Precision.HIGHEST, preferred_element_type=f32,
    ) / (width * n_tp)
    inv_rms[...] = lax.rsqrt(mean + epsilon)
    for copy in third:
        copy.wait_send()


def scale_body(new, inv_rms, gain, new_hbm, norm_hbm, norm, sems):
    rows, width = new.shape
    writes = [pltpu.make_async_copy(new, new_hbm, sems.at[0])]
    writes[0].start()
    piece = rows // 4
    for p in range(4):
        at = pl.ds(p * piece, piece)
        factor = inv_rms[at, :]

        def scale(t, _):
            cols = pl.ds(pl.multiple_of(t * lane, lane), lane)
            norm[at, cols] = (new[at, cols].astype(f32) * factor * gain[:, cols]).astype(bf16)
            return 0

        lax.fori_loop(0, width // lane, scale, 0, unroll=4)
        writes.append(pltpu.make_async_copy(norm.at[at], norm_hbm.at[at], sems.at[p + 1]))
        writes[-1].start()
    for write in writes:
        write.wait()


def shards(n_ctx, n_tp, queries, key_proj, values, residues, decay_rates, skip_weight, stream, norm_gain):
    rows, width = queries.shape
    modes = residues.shape[0]
    n_lane = width // lane
    n_sub = max(1, n_ctx // n_lane)
    part = modes // n_sub
    blocks = n_lane * n_sub
    per_dev = blocks // n_ctx
    chunk = rows // 2
    assert per_dev * n_ctx == blocks and part * n_sub == modes
    forward, inverse = dft_tables(chunk)
    slab = pltpu.VMEM((rows, width), bf16)
    wide = pltpu.VMEM((modes, width), f32)
    line = pltpu.VMEM((1, width), f32)
    dma = pltpu.SemaphoreType.DMA
    whole = pl.BlockSpec(memory_space=pl.ANY)
    near = pl.BlockSpec(memory_space=pltpu.VMEM)
    out = jax.ShapeDtypeStruct((rows, width), bf16)
    args = (
        queries, key_proj, values, residues, decay_rates, skip_weight[None, :], stream,
        jnp.asarray(forward), jnp.asarray(inverse),
    )
    new, inv_rms = pl.pallas_call(
        functools.partial(body, n_ctx, n_tp, n_sub, per_dev, chunk),
        out_shape=(pltpu.VMEM((rows, width), bf16), pltpu.VMEM((rows, lane), f32)),
        in_specs=[whole] * 9,
        out_specs=(near, near),
        scratch_shapes=[
            slab, slab, slab, wide, wide, line, slab,
            pltpu.VMEM((2 * chunk, chunk), bf16), pltpu.VMEM((chunk, 2 * chunk), bf16),
            slab, pltpu.VMEM((chunk, width), bf16), pltpu.VMEM((rows, width), f32),
            pltpu.VMEM((blocks, part, lane), f32),
            pltpu.VMEM((rows // chunk - 1, n_lane, modes, lane), f32),
            pltpu.VMEM((blocks, part, lane), f32),
            pltpu.VMEM((n_ctx, per_dev, part, lane), f32),
            pltpu.VMEM((n_ctx, per_dev, part, lane), f32),
            pltpu.VMEM((blocks, part, lane), f32),
            pltpu.VMEM((rows, lane), f32),
            pltpu.VMEM((n_tp, sub, rows), f32),
            dma((9,)),
            dma((n_ctx,)), dma((n_ctx,)), dma((n_ctx,)), dma((n_ctx,)), dma((n_tp,)), dma((n_tp,)),
        ],
        compiler_params=pltpu.CompilerParams(
            collective_id=0, has_side_effects=True, vmem_limit_bytes=40 * 1024 * 1024
        ),
        cost_estimate=pl.CostEstimate(
            flops=6 * rows * rows * width * 2, bytes_accessed=6 * rows * width * 2, transcendentals=0
        ),
    )(*[pltpu.with_memory_space_constraint(x, pltpu.HBM) for x in args])
    return pl.pallas_call(
        scale_body,
        out_shape=(out, out),
        in_specs=[near] * 3,
        out_specs=(whole, whole),
        scratch_shapes=[slab, dma((5,))],
        compiler_params=pltpu.CompilerParams(vmem_limit_bytes=40 * 1024 * 1024),
        cost_estimate=pl.CostEstimate(flops=2 * rows * width, bytes_accessed=6 * rows * width, transcendentals=0),
    )(new, inv_rms, norm_gain[None, :])


def solution(mesh):
    in_specs = (
        P("ctx", "tp"),
        P("ctx", "tp"),
        P("ctx", "tp"),
        P(None, "tp"),
        P(None, "tp"),
        P("tp"),
        P("ctx", "tp"),
        P("tp"),
    )
    out_specs = (P("ctx", "tp"), P("ctx", "tp"))
    return jax.shard_map(
        functools.partial(shards, mesh.shape["ctx"], mesh.shape["tp"]),
        mesh=mesh, in_specs=in_specs, out_specs=out_specs, check_vma=False,
    )
```

time: 38.8 us -> 26.7 us (0.69)
  local copies, waits for them, and re-layouts: 10.7 us -> 0.01 us
  Pallas kernels: 27 us -> 25.9 us
    unnamed x20 -> x2, local copies, waits for them, and re-layouts: 10.7 us -> 0.01 us
    pallas_call x1 -> x2, Pallas kernels: 27 us -> 25.9 us  [the longest x1 24.5 us: shards(): pl.pallas_call(functools.partial(body, n_ctx, n_tp, n_sub, per_dev, chunk...]
where the time goes in v1:
time: 26.7 us; the launch traced here: 26.5 us
  Pallas kernels  25.9 us (97%)
  between operations  0.66 us (2%)
    pallas_call x1, Pallas kernels, shards(): pl.pallas_call(functools.partial(body, n_ctx, n_tp, n_sub, per_dev, chunk...  24.5 us
    pallas_call x1, Pallas kernels, shards(): pl.pallas_call(scale_body, out_shape=(out, out), in_specs=[near] * 3, out...  1.35 us

profile of v1, /device:TPU:0, one launch (start us, length us, event | category | flops | bytes accessed | tf_op | source)
XLA Modules:
  0.0 26.5 jit_solution(12039433190301068113)
XLA Ops:
  0.6 0.0 copy-start
  0.6 24.5 %shard_map.113 = (bf16[256,2048]{1,0:T(8,128)(2,1)S(1)}, f32[256,128]{1,0:T(8,128)S(1)}) custom-call(bf16[256,2048]{1,0:T(8,128)(2,1)} %q_hbm.1, bf16[256,2048]{1,0:T(8,128)(2,1)} %k_hbm.1, bf16[256,2048]{1,0:T(8,128)(2,1)} %v_hbm.1, f32[16,2048]{1,0:T(8,128)} %res_hbm.1, f32[16,2048]{1,0:T(8,128)} %dec_hbm.1, f32[1,2048]{1,0:T(1,128)} %bitcast.3, ...), custom_call_target="tpu_custom_call" | custom-call | flops 1610612736 | bytes 6291456 | tf_op jit(solution)/shard_map/pallas_call | solution.py:319
  25.2 0.0 copy-done
  25.2 1.4 %shard_map.114 = (bf16[256,2048]{1,0:T(8,128)(2,1)}, bf16[256,2048]{1,0:T(8,128)(2,1)}) custom-call(bf16[256,2048]{1,0:T(8,128)(2,1)S(1)} %get-tuple-element.4.new, f32[256,128]{1,0:T(8,128)S(1)} %get-tuple-element.5.inv_rms, f32[1,2048]{1,0:T(1,128)S(1)} %bitcast.2), custom_call_target="tpu_custom_call" | custom-call | flops 1048576 | bytes 3145728 | tf_op jit(solution)/shard_map/pallas_call | solution.py:346
Async XLA Ops:
  0.6 24.5 %copy-start = (f32[2048]{0:T(1024)S(1)}, f32[2048]{0:T(1024)}, u32[]{:S(2)}) copy-start(f32[2048]{0:T(1024)} %param.17) | copy-start | bytes 24580

commit v2 on v1

--- a/solution.py
+++ b/solution.py
@@ -18,12 +18,18 @@
 bf16 = jnp.bfloat16
 
 
+def tree_sum(terms):
+    while len(terms) > 1:
+        terms = [a + b for a, b in zip(terms[::2], terms[1::2])] + terms[len(terms) // 2 * 2:]
+    return terms[0]
+
+
 def dft_tables(rows):
     freq = np.arange(rows)[:, None]
     pos = np.arange(rows)[None, :]
     angle = math.pi * (((2 * freq + 1) * pos) % (4 * rows)) / (2 * rows)
     forward = np.concatenate([np.cos(angle), -np.sin(angle)], axis=0)
-    inverse = np.concatenate([np.cos(angle).T, -np.sin(angle).T], axis=1) / rows
+    inverse = np.concatenate([np.cos(angle).T, -np.sin(angle).T], axis=0) / rows
     return np.ascontiguousarray(forward.astype(bf16)), np.ascontiguousarray(inverse.astype(bf16))
 
 
@@ -138,31 +144,49 @@
 
     def modal(h, coefs, steps, emit):
         def block(m, z):
-            top = sum(z[1:], z[0])
+            top = tree_sum(list(z))
             z = tuple(a * b for a, b in zip(z, steps))
-            low = sum(z[1:], z[0])
+            low = tree_sum(list(z))
             z = tuple(a * b for a, b in zip(z, steps))
             emit(rows_of(h, m), jnp.concatenate([top, low], axis=0))
             return z
 
         lax.fori_loop(0, chunk // 16, block, tuple(coefs), unroll=True)
 
-    loads["res"].wait()
-
-    def make_taps(t):
-        cols = lanes_of(t)
-        rate = dec[:, cols]
-        weight = res[:, cols]
-        step = jnp.exp(rate * (-float(sub)))
-        steps = [spread(step, n) for n in range(modes)]
-        coefs = [spread(weight, n) * jnp.exp(-spread(rate, n) * sublane) for n in range(modes)]
-
-        def emit(at, value):
-            taps[at, cols] = value.astype(bf16)
-
-        modal(0, coefs, steps, emit)
-
-    loop(0, n_lane, make_taps)
+    for name in ("res", "fwd", "inv", "v", "stream", "skip"):
+        loads[name].wait()
+
+    def local_part(c):
+        for i in range(dft_cols // lane):
+            cols = lanes_of(c * (dft_cols // lane) + i)
+            rate = dec[:, cols]
+            weight = res[:, cols]
+            step = jnp.exp(rate * (-float(sub)))
+            steps = [spread(step, n) for n in range(modes)]
+            coefs = [spread(weight, n) * jnp.exp(-spread(rate, n) * sublane) for n in range(modes)]
+
+            def emit(at, value):
+                taps[at, i * lane:(i + 1) * lane] = value.astype(bf16)
+
+            modal(0, coefs, steps, emit)
+
+        cols = pl.ds(pl.multiple_of(c * dft_cols, dft_cols), dft_cols)
+        table = fwd[...]
+        back = jnp.concatenate([inv[:chunk, :], inv[chunk:, :]], axis=1)
+        g = jnp.dot(table, taps[...], preferred_element_type=f32)
+        gr, gi = g[:chunk], g[chunk:]
+        direct = skip[:, cols]
+        for h in range(n_chunk):
+            at = pl.ds(h * chunk, chunk)
+            part_sig = sig[at, cols]
+            u = jnp.dot(table, part_sig, preferred_element_type=f32)
+            ur, ui = u[:chunk], u[chunk:]
+            prod = jnp.concatenate([ur * gr - ui * gi, ur * gi + ui * gr], axis=0).astype(bf16)
+            value = jnp.dot(back, prod, preferred_element_type=f32) + direct * part_sig.astype(f32)
+            conv[at, cols] = stream[at, cols].astype(f32) + v[at, cols].astype(f32) * value
+
+    n_local = width // dft_cols
+    loop(0, n_local // 2, local_part)
 
     loop(1, n_ctx, lambda d: copy_ends(d).wait_recv())
     got[me] = ends[mine]
@@ -182,24 +206,8 @@
     loop(1, n_ctx, lambda d: copy_starts(d).start())
     states[mine] = starts[me]
 
-    loads["fwd"].wait()
-    loads["inv"].wait()
-
-    def local_conv(c):
-        cols = pl.ds(pl.multiple_of(c * dft_cols, dft_cols), dft_cols)
-        g = jnp.dot(fwd[...], taps[:, cols], preferred_element_type=f32)
-        gr, gi = g[:chunk], g[chunk:]
-        for h in range(n_chunk):
-            at = pl.ds(h * chunk, chunk)
-            u = jnp.dot(fwd[...], sig[at, cols], preferred_element_type=f32)
-            ur, ui = u[:chunk], u[chunk:]
-            prod = jnp.concatenate([ur * gr - ui * gi, ur * gi + ui * gr], axis=0).astype(bf16)
-            conv[at, cols] = jnp.dot(inv[...], prod, preferred_element_type=f32)
-
-    loop(0, width // dft_cols, local_conv)
-
-    for name in ("v", "stream", "skip"):
-        loads[name].wait()
+    loop(n_local // 2, n_local, local_part)
+
     square[...] = jnp.zeros_like(square)
 
     def finish(t):
@@ -210,11 +218,9 @@
         step = jnp.exp(rate * (-float(sub)))
         steps = [spread(step, n) for n in range(modes)]
         heads = [jnp.exp(-spread(rate, n) * (sublane + 1.0)) for n in range(modes)]
-        direct = skip[:, cols]
 
         def emit(at, value):
-            value = value + conv[at, cols] + direct * sig[at, cols].astype(f32)
-            out = (stream[at, cols].astype(f32) + v[at, cols].astype(f32) * value).astype(bf16)
+            out = (conv[at, cols] + v[at, cols].astype(f32) * value).astype(bf16)
             new[at, cols] = out
             out = out.astype(f32)
             square[at, :] += out * out
@@ -323,8 +329,8 @@
         out_specs=(near, near),
         scratch_shapes=[
             slab, slab, slab, wide, wide, line, slab,
-            pltpu.VMEM((2 * chunk, chunk), bf16), pltpu.VMEM((chunk, 2 * chunk), bf16),
-            slab, pltpu.VMEM((chunk, width), bf16), pltpu.VMEM((rows, width), f32),
+            pltpu.VMEM((2 * chunk, chunk), bf16), pltpu.VMEM((2 * chunk, chunk), bf16),
+            slab, pltpu.VMEM((chunk, dft_cols), bf16), pltpu.VMEM((rows, width), f32),
             pltpu.VMEM((blocks, part, lane), f32),
             pltpu.VMEM((rows // chunk - 1, n_lane, modes, lane), f32),
             pltpu.VMEM((blocks, part, lane), f32),

time: 26.7 us -> 26.2 us (0.981)
  Pallas kernels: 25.9 us -> 25.4 us
    pallas_call x1, Pallas kernels: 24.5 us -> 24 us  [shards(): pl.pallas_call(functools.partial(body, n_ctx, n_tp, n_sub, per_dev, chunk...]
where the time goes in v2:
time: 26.2 us; the launch traced here: 26.1 us
  Pallas kernels  25.4 us (97%)
  between operations  0.66 us (3%)
    pallas_call x1, Pallas kernels, shards(): pl.pallas_call(functools.partial(body, n_ctx, n_tp, n_sub, per_dev, chunk...  24 us
    pallas_call x1, Pallas kernels, shards(): pl.pallas_call(scale_body, out_shape=(out, out), in_specs=[near] * 3, out...  1.35 us

profile of v2, /device:TPU:0, one launch (start us, length us, event | category | flops | bytes accessed | tf_op | source)
XLA Modules:
  0.0 26.1 jit_solution(10939832234625322923)
XLA Ops:
  0.6 0.0 copy-start
  0.6 24.0 %shard_map.113 = (bf16[256,2048]{1,0:T(8,128)(2,1)S(1)}, f32[256,128]{1,0:T(8,128)S(1)}) custom-call(bf16[256,2048]{1,0:T(8,128)(2,1)} %q_hbm.1, bf16[256,2048]{1,0:T(8,128)(2,1)} %k_hbm.1, bf16[256,2048]{1,0:T(8,128)(2,1)} %v_hbm.1, f32[16,2048]{1,0:T(8,128)} %res_hbm.1, f32[16,2048]{1,0:T(8,128)} %dec_hbm.1, f32[1,2048]{1,0:T(1,128)} %bitcast.3, ...), custom_call_target="tpu_custom_call" | custom-call | flops 1610612736 | bytes 6291456 | tf_op jit(solution)/shard_map/pallas_call | solution.py:325
  24.7 0.0 copy-done
  24.7 1.4 %shard_map.114 = (bf16[256,2048]{1,0:T(8,128)(2,1)}, bf16[256,2048]{1,0:T(8,128)(2,1)}) custom-call(bf16[256,2048]{1,0:T(8,128)(2,1)S(1)} %get-tuple-element.4.new, f32[256,128]{1,0:T(8,128)S(1)} %get-tuple-element.5.inv_rms, f32[1,2048]{1,0:T(1,128)S(1)} %bitcast.2), custom_call_target="tpu_custom_call" | custom-call | flops 1048576 | bytes 3145728 | tf_op jit(solution)/shard_map/pallas_call | solution.py:352
Async XLA Ops:
  0.6 24.1 %copy-start = (f32[2048]{0:T(1024)S(1)}, f32[2048]{0:T(1024)}, u32[]{:S(2)}) copy-start(f32[2048]{0:T(1024)} %param.17) | copy-start | bytes 24580

commit v3 on v2

--- a/solution.py
+++ b/solution.py
@@ -39,7 +39,7 @@
     new, inv_rms,
     q, k, v, res, dec, skip, stream, fwd, inv,
     sig, taps, conv, ends, mids, decay_pow, got, starts, states, square, row_sums,
-    in_sem, send1, recv1, send2, recv2, send3, recv3,
+    in_sem, gate_sem, send1, recv1, send2, recv2, send3, recv3,
 ):
     rows, width = q.shape
     modes = res.shape[0]
@@ -49,15 +49,34 @@
     me = lax.axis_index("ctx")
     tp = lax.axis_index("tp")
 
-    loads = {}
+    share_width = width // n_ctx if n_sub == 1 else width
+
+    def gate_loads(d):
+        if n_sub == 1:
+            first = lax.rem(me + d, n_ctx) * share_width
+            cols = pl.ds(pl.multiple_of(first, share_width), share_width)
+        else:
+            cols = pl.ds(0, width)
+        return [
+            pltpu.make_async_copy(src.at[:, cols], dst.at[:, cols], gate_sem.at[i, d])
+            for i, (src, dst) in enumerate(((q_hbm, q), (k_hbm, k)))
+        ]
+
+    def start_gates(d):
+        for copy in gate_loads(d):
+            copy.start()
+
+    def wait_gates(d):
+        for copy in gate_loads(d):
+            copy.wait()
+
     order = [
-        ("dec", dec_hbm, dec), ("q", q_hbm, q), ("k", k_hbm, k), ("res", res_hbm, res),
-        ("fwd", fwd_hbm, fwd), ("inv", inv_hbm, inv), ("v", v_hbm, v),
-        ("stream", str_hbm, stream), ("skip", skip_hbm, skip),
+        (dec_hbm, dec), (res_hbm, res), (fwd_hbm, fwd), (inv_hbm, inv), (skip_hbm, skip),
+        (v_hbm, v), (str_hbm, stream),
     ]
-    for i, (name, src, dst) in enumerate(order):
-        loads[name] = pltpu.make_async_copy(src, dst, in_sem.at[i])
-        loads[name].start()
+    loads = [pltpu.make_async_copy(src, dst, in_sem.at[i]) for i, (src, dst) in enumerate(order)]
+    loads[0].start()
+    start_gates(1)
 
     barrier = pltpu.get_barrier_semaphore()
     for d in range(1, n_ctx):
@@ -75,9 +94,6 @@
 
     def rows_of(h, m):
         return pl.ds(pl.multiple_of(h * chunk + m * 16, 16), 16)
-
-    for name in ("dec", "q", "k"):
-        loads[name].wait()
 
     def end_states(t):
         cols = lanes_of(t)
@@ -114,6 +130,10 @@
 
         lax.fori_loop(first, last, run, 0)
 
+    if n_sub == 1:
+        loop(2, n_ctx, start_gates)
+        start_gates(0)
+    loads[0].wait()
     mine = pl.ds(me * per_dev, per_dev)
 
     def copy_ends(d):
@@ -125,9 +145,13 @@
 
     if n_sub == 1:
         def share(d):
-            loop(0, per_dev, lambda i: end_states(lax.rem(me + d, n_ctx) * per_dev + i))
+            wait_gates(d)
+            for i in range(per_dev):
+                end_states(lax.rem(me + d, n_ctx) * per_dev + i)
 
         share(1)
+        for copy in loads[1:]:
+            copy.start()
         pl.semaphore_wait(barrier, n_ctx - 1 + n_tp - 1)
         copy_ends(1).start()
 
@@ -138,6 +162,9 @@
         loop(2, n_ctx, share_and_send)
         share(0)
     else:
+        wait_gates(1)
+        for copy in loads[1:]:
+            copy.start()
         loop(0, n_lane, end_states)
         pl.semaphore_wait(barrier, n_ctx - 1 + n_tp - 1)
         loop(1, n_ctx, lambda d: copy_ends(d).start())
@@ -153,8 +180,8 @@
 
         lax.fori_loop(0, chunk // 16, block, tuple(coefs), unroll=True)
 
-    for name in ("res", "fwd", "inv", "v", "stream", "skip"):
-        loads[name].wait()
+    for copy in loads[1:]:
+        copy.wait()
 
     def local_part(c):
         for i in range(dft_cols // lane):
@@ -233,7 +260,8 @@
     if n_sub == 1:
         def finish_share(d):
             frm = lax.rem(me - d + n_ctx, n_ctx)
-            loop(0, per_dev, lambda i: finish(frm * per_dev + i))
+            for i in range(per_dev):
+                finish(frm * per_dev + i)
 
         def wait_and_finish(d):
             frm = lax.rem(me - d + n_ctx, n_ctx)
@@ -339,7 +367,7 @@
             pltpu.VMEM((blocks, part, lane), f32),
             pltpu.VMEM((rows, lane), f32),
             pltpu.VMEM((n_tp, sub, rows), f32),
-            dma((9,)),
+            dma((7,)), dma((2, n_ctx)),
             dma((n_ctx,)), dma((n_ctx,)), dma((n_ctx,)), dma((n_ctx,)), dma((n_tp,)), dma((n_tp,)),
         ],
         compiler_params=pltpu.CompilerParams(

time: 26.2 us -> 26.2 us (level)
  no operation moved by 1% of the time
where the time goes in v3:
time: 26.2 us; the launch traced here: 26 us
  Pallas kernels  25.4 us (97%)
  between operations  0.66 us (3%)
    pallas_call x1, Pallas kernels, shards(): pl.pallas_call(functools.partial(body, n_ctx, n_tp, n_sub, per_dev, chunk...  24 us
    pallas_call x1, Pallas kernels, shards(): pl.pallas_call(scale_body, out_shape=(out, out), in_specs=[near] * 3, out...  1.35 us

profile of v3, /device:TPU:0, one launch (start us, length us, event | category | flops | bytes accessed | tf_op | source)
XLA Modules:
  0.0 26.0 jit_solution(1656989579249215600)
XLA Ops:
  0.6 0.0 copy-start
  0.6 24.0 %shard_map.113 = (bf16[256,2048]{1,0:T(8,128)(2,1)S(1)}, f32[256,128]{1,0:T(8,128)S(1)}) custom-call(bf16[256,2048]{1,0:T(8,128)(2,1)} %q_hbm.1, bf16[256,2048]{1,0:T(8,128)(2,1)} %k_hbm.1, bf16[256,2048]{1,0:T(8,128)(2,1)} %v_hbm.1, f32[16,2048]{1,0:T(8,128)} %res_hbm.1, f32[16,2048]{1,0:T(8,128)} %dec_hbm.1, f32[1,2048]{1,0:T(1,128)} %bitcast.3, ...), custom_call_target="tpu_custom_call" | custom-call | flops 1610612736 | bytes 6291456 | tf_op jit(solution)/shard_map/pallas_call | solution.py:353
  24.7 0.0 copy-done
  24.7 1.4 %shard_map.114 = (bf16[256,2048]{1,0:T(8,128)(2,1)}, bf16[256,2048]{1,0:T(8,128)(2,1)}) custom-call(bf16[256,2048]{1,0:T(8,128)(2,1)S(1)} %get-tuple-element.4.new, f32[256,128]{1,0:T(8,128)S(1)} %get-tuple-element.5.inv_rms, f32[1,2048]{1,0:T(1,128)S(1)} %bitcast.2), custom_call_target="tpu_custom_call" | custom-call | flops 1048576 | bytes 3145728 | tf_op jit(solution)/shard_map/pallas_call | solution.py:380
Async XLA Ops:
  0.6 24.1 %copy-start = (f32[2048]{0:T(1024)S(1)}, f32[2048]{0:T(1024)}, u32[]{:S(2)}) copy-start(f32[2048]{0:T(1024)} %param.17) | copy-start | bytes 24580

commit v4 on v2

--- a/solution.py
+++ b/solution.py
@@ -34,34 +34,63 @@
 
 
 def body(
-    n_ctx, n_tp, n_sub, per_dev, chunk,
+    n_ctx, n_tp, piece, chunk,
     q_hbm, k_hbm, v_hbm, res_hbm, dec_hbm, skip_hbm, str_hbm, fwd_hbm, inv_hbm,
     new, inv_rms,
     q, k, v, res, dec, skip, stream, fwd, inv,
-    sig, taps, conv, ends, mids, decay_pow, got, starts, states, square, row_sums,
-    in_sem, send1, recv1, send2, recv2, send3, recv3,
+    sig, taps, conv, ends, mids, decay_pow, got, chain_in, chain_out, starts, states, square, row_sums,
+    in_sem, gate_sem, send1, recv1, send2, recv2, send3, recv3, send4, recv4,
 ):
     rows, width = q.shape
     modes = res.shape[0]
     n_lane = width // lane
     n_chunk = rows // chunk
-    part = modes // n_sub
     me = lax.axis_index("ctx")
     tp = lax.axis_index("tp")
-
-    loads = {}
+    odd = lax.rem(me, 2)
+    pair = me // 2
+    n_pair = n_ctx // 2
+    mate = me + 1 - 2 * odd
+    half = n_lane // 2
+    n_piece = half // piece
+    own_first = odd * half
+    mate_first = half - own_first
+
+    width_piece = piece * lane
+
+    def tile_of(g):
+        return lax.rem(mate_first + g * piece, n_lane)
+
+    def gate_loads(g):
+        cols = pl.ds(pl.multiple_of(tile_of(g) * lane, width_piece), width_piece)
+        return [
+            pltpu.make_async_copy(src.at[:, cols], dst.at[:, cols], gate_sem.at[i, g])
+            for i, (src, dst) in enumerate(((q_hbm, q), (k_hbm, k)))
+        ]
+
+    def start_gates(g):
+        for copy in gate_loads(g):
+            copy.start()
+
+    def wait_gates(g):
+        for copy in gate_loads(g):
+            copy.wait()
+
     order = [
-        ("dec", dec_hbm, dec), ("q", q_hbm, q), ("k", k_hbm, k), ("res", res_hbm, res),
-        ("fwd", fwd_hbm, fwd), ("inv", inv_hbm, inv), ("v", v_hbm, v),
-        ("stream", str_hbm, stream), ("skip", skip_hbm, skip),
+        (dec_hbm, dec), (res_hbm, res), (fwd_hbm, fwd), (inv_hbm, inv), (skip_hbm, skip),
+        (v_hbm, v), (str_hbm, stream),
     ]
-    for i, (name, src, dst) in enumerate(order):
-        loads[name] = pltpu.make_async_copy(src, dst, in_sem.at[i])
-        loads[name].start()
+    loads = [pltpu.make_async_copy(src, dst, in_sem.at[i]) for i, (src, dst) in enumerate(order)]
+    loads[0].start()
+    start_gates(0)
 
     barrier = pltpu.get_barrier_semaphore()
-    for d in range(1, n_ctx):
-        pl.semaphore_signal(barrier, inc=1, device_id={"ctx": lax.rem(me + d, n_ctx)}, device_id_type=MESH)
+    pl.semaphore_signal(barrier, inc=1, device_id={"ctx": mate}, device_id_type=MESH)
+
+    @pl.when(pair > 0)
+    def _():
+        pl.semaphore_signal(barrier, inc=1, device_id={"ctx": lax.rem(me + n_ctx - 2, n_ctx)}, device_id_type=MESH)
+
     for d in range(1, n_tp):
         pl.semaphore_signal(barrier, inc=1, device_id={"tp": lax.rem(tp + d, n_tp)}, device_id_type=MESH)
 
@@ -75,9 +104,6 @@
 
     def rows_of(h, m):
         return pl.ds(pl.multiple_of(h * chunk + m * 16, 16), 16)
-
-    for name in ("dec", "q", "k"):
-        loads[name].wait()
 
     def end_states(t):
         cols = lanes_of(t)
@@ -103,9 +129,8 @@
             if h < n_chunk - 1:
                 mids[h, t] = total
         power = jnp.exp(rate * (-float(rows)))
-        for g in range(n_sub):
-            ends[t * n_sub + g] = total[g * part:(g + 1) * part]
-            decay_pow[t * n_sub + g] = power[g * part:(g + 1) * part]
+        ends[t] = total
+        decay_pow[t] = power
 
     def loop(first, last, step):
         def run(i, _):
@@ -114,33 +139,48 @@
 
         lax.fori_loop(first, last, run, 0)
 
-    mine = pl.ds(me * per_dev, per_dev)
-
-    def copy_ends(d):
-        to = lax.rem(me + d, n_ctx)
+    loop(1, 2 * n_piece, start_gates)
+    loads[0].wait()
+
+    def piece_of(first, g):
+        return pl.ds(first + g * piece, piece)
+
+    def copy_ends(g):
         return pltpu.make_async_remote_copy(
-            src_ref=ends.at[pl.ds(to * per_dev, per_dev)], dst_ref=got.at[me],
-            send_sem=send1.at[d], recv_sem=recv1.at[d], device_id={"ctx": to}, device_id_type=MESH,
+            src_ref=ends.at[piece_of(mate_first, g)], dst_ref=got.at[piece_of(0, g)],
+            send_sem=send1.at[g], recv_sem=recv1.at[g], device_id={"ctx": mate}, device_id_type=MESH,
         )
 
-    if n_sub == 1:
-        def share(d):
-            loop(0, per_dev, lambda i: end_states(lax.rem(me + d, n_ctx) * per_dev + i))
-
-        share(1)
-        pl.semaphore_wait(barrier, n_ctx - 1 + n_tp - 1)
-        copy_ends(1).start()
-
-        def share_and_send(d):
-            share(d)
-            copy_ends(d).start()
-
-        loop(2, n_ctx, share_and_send)
-        share(0)
-    else:
-        loop(0, n_lane, end_states)
-        pl.semaphore_wait(barrier, n_ctx - 1 + n_tp - 1)
-        loop(1, n_ctx, lambda d: copy_ends(d).start())
+    def copy_chain(g):
+        return pltpu.make_async_remote_copy(
+            src_ref=chain_out.at[piece_of(0, g)], dst_ref=chain_in.at[piece_of(0, g)],
+            send_sem=send4.at[g], recv_sem=recv4.at[g],
+            device_id={"ctx": lax.rem(me + 2, n_ctx)}, device_id_type=MESH,
+        )
+
+    def copy_starts(g):
+        return pltpu.make_async_remote_copy(
+            src_ref=starts.at[piece_of(0, g)], dst_ref=states.at[piece_of(own_first, g)],
+            send_sem=send2.at[g], recv_sem=recv2.at[g], device_id={"ctx": mate}, device_id_type=MESH,
+        )
+
+    def piece_ends(g):
+        wait_gates(g)
+        for i in range(piece):
+            end_states(tile_of(g) + i)
+
+    piece_ends(0)
+    for copy in loads[1:]:
+        copy.start()
+    pl.semaphore_wait(barrier, n_tp + jnp.minimum(n_pair - 1 - pair, 1))
+    copy_ends(0).start()
+
+    def ends_and_send(g):
+        piece_ends(g)
+        copy_ends(g).start()
+
+    loop(1, n_piece, ends_and_send)
+    loop(n_piece, 2 * n_piece, piece_ends)
 
     def modal(h, coefs, steps, emit):
         def block(m, z):
@@ -153,8 +193,8 @@
 
         lax.fori_loop(0, chunk // 16, block, tuple(coefs), unroll=True)
 
-    for name in ("res", "fwd", "inv", "v", "stream", "skip"):
-        loads[name].wait()
+    for copy in loads[1:]:
+        copy.wait()
 
     def local_part(c):
         for i in range(dft_cols // lane):
@@ -186,34 +226,47 @@
             conv[at, cols] = stream[at, cols].astype(f32) + v[at, cols].astype(f32) * value
 
     n_local = width // dft_cols
-    loop(0, n_local // 2, local_part)
-
-    loop(1, n_ctx, lambda d: copy_ends(d).wait_recv())
-    got[me] = ends[mine]
-    power = decay_pow[mine]
-    running = jnp.zeros_like(power)
-    for j in range(n_ctx):
-        starts[j] = running
-        running = running * power + got[j]
-
-    def copy_starts(d):
-        to = lax.rem(me + d, n_ctx)
-        return pltpu.make_async_remote_copy(
-            src_ref=starts.at[to], dst_ref=states.at[mine],
-            send_sem=send2.at[d], recv_sem=recv2.at[d], device_id={"ctx": to}, device_id_type=MESH,
-        )
-
-    loop(1, n_ctx, lambda d: copy_starts(d).start())
-    states[mine] = starts[me]
-
-    loop(n_local // 2, n_local, local_part)
+    before = jnp.minimum(2 * pair, n_local)
+    loop(0, before, local_part)
+
+    @pl.when(pair == 0)
+    def _():
+        chain_in[...] = jnp.zeros_like(chain_in)
+
+    def pass_on(g):
+        copy_ends(g).wait_recv()
+
+        @pl.when(pair > 0)
+        def _():
+            copy_chain(g).wait_recv()
+
+        here = piece_of(0, g)
+        own = piece_of(own_first, g)
+        power = decay_pow[own]
+        is_odd = odd == 1
+        first_end = jnp.where(is_odd, got[here], ends[own])
+        last_end = jnp.where(is_odd, ends[own], got[here])
+        even_start = chain_in[here]
+        odd_start = power * even_start + first_end
+        chain_out[here] = power * odd_start + last_end
+
+        @pl.when(pair < n_pair - 1)
+        def _():
+            copy_chain(g).start()
+
+        states[own] = jnp.where(is_odd, odd_start, even_start)
+        starts[here] = jnp.where(is_odd, even_start, odd_start)
+        copy_starts(g).start()
+
+    loop(0, n_piece, pass_on)
+    loop(before, n_local, local_part)
 
     square[...] = jnp.zeros_like(square)
 
     def finish(t):
         cols = lanes_of(t)
         rate = dec[:, cols]
-        state = jnp.concatenate([states[t * n_sub + g] for g in range(n_sub)], axis=0)
+        state = states[t]
         weight = res[:, cols]
         step = jnp.exp(rate * (-float(sub)))
         steps = [spread(step, n) for n in range(modes)]
@@ -230,24 +283,20 @@
             now = now * weight
             modal(h, [spread(now, n) * w for n, w in enumerate(heads)], steps, emit)
 
-    if n_sub == 1:
-        def finish_share(d):
-            frm = lax.rem(me - d + n_ctx, n_ctx)
-            loop(0, per_dev, lambda i: finish(frm * per_dev + i))
-
-        def wait_and_finish(d):
-            frm = lax.rem(me - d + n_ctx, n_ctx)
-            pltpu.make_async_remote_copy(
-                src_ref=starts.at[me], dst_ref=states.at[pl.ds(frm * per_dev, per_dev)],
-                send_sem=send2.at[d], recv_sem=recv2.at[d], device_id={"ctx": frm}, device_id_type=MESH,
-            ).wait_recv()
-            finish_share(d)
-
-        finish_share(0)
-        loop(1, n_ctx, wait_and_finish)
-    else:
-        loop(1, n_ctx, lambda d: copy_starts(d).wait_recv())
-        loop(0, n_lane, finish)
+    def finish_own(g):
+        for i in range(piece):
+            finish(own_first + g * piece + i)
+
+    def finish_mate(g):
+        pltpu.make_async_remote_copy(
+            src_ref=starts.at[piece_of(0, g)], dst_ref=states.at[piece_of(mate_first, g)],
+            send_sem=send2.at[g], recv_sem=recv2.at[g], device_id={"ctx": mate}, device_id_type=MESH,
+        ).wait_recv()
+        for i in range(piece):
+            finish(mate_first + g * piece + i)
+
+    loop(0, n_piece, finish_own)
+    loop(0, n_piece, finish_mate)
 
     ones = jnp.ones((sub, lane), f32)
     row_sums[tp] = lax.dot_general(
@@ -263,8 +312,13 @@
         )
         copy.start()
         third.append(copy)
-    loop(1, n_ctx, lambda d: copy_ends(d).wait_send())
-    loop(1, n_ctx, lambda d: copy_starts(d).wait_send())
+    loop(0, n_piece, lambda g: copy_ends(g).wait_send())
+    loop(0, n_piece, lambda g: copy_starts(g).wait_send())
+
+    @pl.when(pair < n_pair - 1)
+    def _():
+        loop(0, n_piece, lambda g: copy_chain(g).wait_send())
+
     for copy in third:
         copy.wait_recv()
     total = row_sums[0]
@@ -304,12 +358,11 @@
     rows, width = queries.shape
     modes = residues.shape[0]
     n_lane = width // lane
-    n_sub = max(1, n_ctx // n_lane)
-    part = modes // n_sub
-    blocks = n_lane * n_sub
-    per_dev = blocks // n_ctx
+    half = n_lane // 2
+    piece = 2
+    n_piece = half // piece
     chunk = rows // 2
-    assert per_dev * n_ctx == blocks and part * n_sub == modes
+    assert n_ctx % 2 == 0 and n_piece * piece * 2 == n_lane
     forward, inverse = dft_tables(chunk)
     slab = pltpu.VMEM((rows, width), bf16)
     wide = pltpu.VMEM((modes, width), f32)
@@ -323,7 +376,7 @@
         jnp.asarray(forward), jnp.asarray(inverse),
     )
     new, inv_rms = pl.pallas_call(
-        functools.partial(body, n_ctx, n_tp, n_sub, per_dev, chunk),
+        functools.partial(body, n_ctx, n_tp, piece, chunk),
         out_shape=(pltpu.VMEM((rows, width), bf16), pltpu.VMEM((rows, lane), f32)),
         in_specs=[whole] * 9,
         out_specs=(near, near),
@@ -331,16 +384,19 @@
             slab, slab, slab, wide, wide, line, slab,
             pltpu.VMEM((2 * chunk, chunk), bf16), pltpu.VMEM((2 * chunk, chunk), bf16),
             slab, pltpu.VMEM((chunk, dft_cols), bf16), pltpu.VMEM((rows, width), f32),
-            pltpu.VMEM((blocks, part, lane), f32),
+            pltpu.VMEM((n_lane, modes, lane), f32),
             pltpu.VMEM((rows // chunk - 1, n_lane, modes, lane), f32),
-            pltpu.VMEM((blocks, part, lane), f32),
-            pltpu.VMEM((n_ctx, per_dev, part, lane), f32),
-            pltpu.VMEM((n_ctx, per_dev, part, lane), f32),
-            pltpu.VMEM((blocks, part, lane), f32),
+            pltpu.VMEM((n_lane, modes, lane), f32),
+            pltpu.VMEM((half, modes, lane), f32),
+            pltpu.VMEM((half, modes, lane), f32),
+            pltpu.VMEM((half, modes, lane), f32),
+            pltpu.VMEM((half, modes, lane), f32),
+            pltpu.VMEM((n_lane, modes, lane), f32),
             pltpu.VMEM((rows, lane), f32),
             pltpu.VMEM((n_tp, sub, rows), f32),
-            dma((9,)),
-            dma((n_ctx,)), dma((n_ctx,)), dma((n_ctx,)), dma((n_ctx,)), dma((n_tp,)), dma((n_tp,)),
+            dma((7,)), dma((2, 2 * n_piece)),
+            dma((n_piece,)), dma((n_piece,)), dma((n_piece,)), dma((n_piece,)),
+            dma((n_tp,)), dma((n_tp,)), dma((n_piece,)), dma((n_piece,)),
         ],
         compiler_params=pltpu.CompilerParams(
             collective_id=0, has_side_effects=True, vmem_limit_bytes=40 * 1024 * 1024

time: 26.2 us -> 23.9 us (0.912)
  the two profiles are of different devices: /device:TPU:0 before, /device:TPU:25 now
where the time goes in v4:
time: 23.9 us; the launch traced here: 23.7 us
  Pallas kernels  23 us (96%)
  between operations  0.66 us (3%)
    pallas_call x1, Pallas kernels, shards(): pl.pallas_call(functools.partial(body, n_ctx, n_tp, piece, chunk), out_sh...  21.7 us
    pallas_call x1, Pallas kernels, shards(): pl.pallas_call(scale_body, out_shape=(out, out), in_specs=[near] * 3, out...  1.35 us

profile of v4, /device:TPU:25, one launch (start us, length us, event | category | flops | bytes accessed | tf_op | source)
XLA Modules:
  0.0 23.7 jit_solution(5409265439763314535)
XLA Ops:
  0.6 0.0 copy-start
  0.6 21.7 %shard_map.113 = (bf16[256,2048]{1,0:T(8,128)(2,1)S(1)}, f32[256,128]{1,0:T(8,128)S(1)}) custom-call(bf16[256,2048]{1,0:T(8,128)(2,1)} %q_hbm.1, bf16[256,2048]{1,0:T(8,128)(2,1)} %k_hbm.1, bf16[256,2048]{1,0:T(8,128)(2,1)} %v_hbm.1, f32[16,2048]{1,0:T(8,128)} %res_hbm.1, f32[16,2048]{1,0:T(8,128)} %dec_hbm.1, f32[1,2048]{1,0:T(1,128)} %bitcast.3, ...), custom_call_target="tpu_custom_call" | custom-call | flops 1610612736 | bytes 6291456 | tf_op jit(solution)/shard_map/pallas_call | solution.py:378
  22.3 0.0 copy-done
  22.4 1.4 %shard_map.114 = (bf16[256,2048]{1,0:T(8,128)(2,1)}, bf16[256,2048]{1,0:T(8,128)(2,1)}) custom-call(bf16[256,2048]{1,0:T(8,128)(2,1)S(1)} %get-tuple-element.4.new, f32[256,128]{1,0:T(8,128)S(1)} %get-tuple-element.5.inv_rms, f32[1,2048]{1,0:T(1,128)S(1)} %bitcast.2), custom_call_target="tpu_custom_call" | custom-call | flops 1048576 | bytes 3145728 | tf_op jit(solution)/shard_map/pallas_call | solution.py:408
Async XLA Ops:
  0.6 21.7 %copy-start = (f32[2048]{0:T(1024)S(1)}, f32[2048]{0:T(1024)}, u32[]{:S(2)}) copy-start(f32[2048]{0:T(1024)} %param.17) | copy-start | bytes 24580

commit v5 on v4

--- a/solution.py
+++ b/solution.py
@@ -226,7 +226,7 @@
             conv[at, cols] = stream[at, cols].astype(f32) + v[at, cols].astype(f32) * value
 
     n_local = width // dft_cols
-    before = jnp.minimum(2 * pair, n_local)
+    before = jnp.minimum(jnp.where(pair < n_pair - 1, pair, 2 * pair), n_local)
     loop(0, before, local_part)
 
     @pl.when(pair == 0)

time: 23.9 us -> 24.2 us (1.013)
  the two profiles are of different devices: /device:TPU:25 before, /device:TPU:17 now
where the time goes in v5:
time: 24.2 us; the launch traced here: 24 us
  Pallas kernels  23.3 us (96%)
  between operations  0.66 us (3%)
    pallas_call x1, Pallas kernels, shards(): pl.pallas_call(functools.partial(body, n_ctx, n_tp, piece, chunk), out_sh...  22 us
    pallas_call x1, Pallas kernels, shards(): pl.pallas_call(scale_body, out_shape=(out, out), in_specs=[near] * 3, out...  1.35 us

profile of v5, /device:TPU:17, one launch (start us, length us, event | category | flops | bytes accessed | tf_op | source)
XLA Modules:
  0.0 24.0 jit_solution(6676343423062629585)
XLA Ops:
  0.6 0.0 copy-start
  0.6 22.0 %shard_map.113 = (bf16[256,2048]{1,0:T(8,128)(2,1)S(1)}, f32[256,128]{1,0:T(8,128)S(1)}) custom-call(bf16[256,2048]{1,0:T(8,128)(2,1)} %q_hbm.1, bf16[256,2048]{1,0:T(8,128)(2,1)} %k_hbm.1, bf16[256,2048]{1,0:T(8,128)(2,1)} %v_hbm.1, f32[16,2048]{1,0:T(8,128)} %res_hbm.1, f32[16,2048]{1,0:T(8,128)} %dec_hbm.1, f32[1,2048]{1,0:T(1,128)} %bitcast.3, ...), custom_call_target="tpu_custom_call" | custom-call | flops 1610612736 | bytes 6291456 | tf_op jit(solution)/shard_map/pallas_call | solution.py:378
  22.6 0.0 copy-done
  22.7 1.4 %shard_map.114 = (bf16[256,2048]{1,0:T(8,128)(2,1)}, bf16[256,2048]{1,0:T(8,128)(2,1)}) custom-call(bf16[256,2048]{1,0:T(8,128)(2,1)S(1)} %get-tuple-element.4.new, f32[256,128]{1,0:T(8,128)S(1)} %get-tuple-element.5.inv_rms, f32[1,2048]{1,0:T(1,128)S(1)} %bitcast.2), custom_call_target="tpu_custom_call" | custom-call | flops 1048576 | bytes 3145728 | tf_op jit(solution)/shard_map/pallas_call | solution.py:408
Async XLA Ops:
  0.6 22.0 %copy-start = (f32[2048]{0:T(1024)S(1)}, f32[2048]{0:T(1024)}, u32[]{:S(2)}) copy-start(f32[2048]{0:T(1024)} %param.17) | copy-start | bytes 24580
